TPU v7x, 512 devices: a whole 4x4x16 slice. The times are simulated.
512 devices in a mesh: dp: 16 (over z), expert: 32 (over y, x, core).
Axes of the slice: x: 4, y: 4, z: 16, core: 2. Of those that a mesh axis runs over, the one named last changes fastest.
Arguments:
- tokens: bfloat16 [65536, 1024], P(('dp', 'expert')), may hold values from -6 to 6
- grad_out: bfloat16 [65536, 1024], P(('dp', 'expert')), may hold values from -6 to 6
- expert_ids: int32 [65536, 2], P(('dp', 'expert')), may hold values from 0 to 31, all different within a row; in each aligned block of 128 rows (0 to 127, 128 to 255, ...) at most 16 rows name the same one
- route_probs: bfloat16 [65536, 2], P(('dp', 'expert')), may hold values from 0.19921875 to 1
- gate_up_weight: bfloat16 [1024, 32, 1536], P('dp', 'expert'), may hold values from -0.1875 to 0.1875
- down_weight: bfloat16 [32, 768, 1024], P('expert'), may hold values from -0.21875 to 0.21875
- gate_up_scale_index: int32 [8, 32, 2], P(None, 'expert'), may hold values from 0 to 15
- down_scale_index: int32 [32, 6], P('expert'), may hold values from 0 to 15
- scale_table: float32 [16], replicated, may hold values from 0.5 to 2
Outputs:
- token_grad: bfloat16 [65536, 1024], P(('dp', 'expert'))
- prob_grad: float32 [65536, 2], P(('dp', 'expert'))
- gate_up_grad: bfloat16 [1024, 32, 1536], P('dp', 'expert')
- down_grad: bfloat16 [32, 768, 1024], P('expert')
Inputs may be any that keep to these rules, and one draw needn't show every extreme that they name: `expert_ids`: each row names two different experts. The 128 rows of one device name one expert at most 16 times, and in every draw some device's rows name some expert exactly 16 times.
All inputs are finite; a program needn't handle non-finite values.
Results may differ from a plain program's by a relative error of at most 0.022.
Values may be sent and summed in bfloat16 or wider, within the bound.
No kernel may reach another device: no remote copies, remote signals or barrier semaphores. Data moves between devices by JAX's collectives and lax.ppermute only.
A program may use at most 64 MiB of HBM per device.

v0:
```python
import jax
import jax.numpy as jnp
from jax import lax
from jax.sharding import PartitionSpec as P

QBLOCK = 128


def lookup(level_index, level_table):
    onehot = (level_index[..., None] == jnp.arange(level_table.shape[0], dtype=jnp.int32)).astype(
        level_table.dtype
    )
    return jnp.sum(onehot * level_table, axis=-1)


def slot_tables(routes, experts, capacity):
    flat_routes = routes.reshape(-1)
    expert_hits = (flat_routes[:, None] == jnp.arange(experts, dtype=jnp.int32)[None, :]).astype(
        jnp.int32
    )
    place = jnp.arange(flat_routes.shape[0], dtype=jnp.int32)
    earlier = (place[None, :] < place[:, None]).astype(jnp.bfloat16)
    before = jnp.dot(
        earlier, expert_hits.astype(jnp.bfloat16), preferred_element_type=jnp.float32
    ).astype(jnp.int32)
    slot_rank = jnp.sum(before * expert_hits, axis=1)
    destination = flat_routes * capacity + slot_rank
    table_hits = destination[:, None] == jnp.arange(experts * capacity, dtype=jnp.int32)[None, :]
    return table_hits.astype(jnp.float32).reshape(routes.shape[0], 2, experts * capacity)


def body(
    tokens,
    grad_out,
    expert_ids,
    route_probs,
    gate_up_weight,
    down_weight,
    gate_up_scale_index,
    down_scale_index,
    scale_table,
):
    high = lax.Precision.HIGHEST
    f32 = jnp.float32
    groups = lax.axis_size("expert")
    tok_dev = tokens.shape[0]
    model_width = tokens.shape[1]
    per_device = down_weight.shape[0]
    hidden = down_weight.shape[1]
    experts = per_device * groups
    capacity = 4 * tok_dev // experts
    slots_all = experts * capacity
    slot_hits = slot_tables(expert_ids, experts, capacity)
    either = (slot_hits[:, 0] + slot_hits[:, 1]).astype(jnp.bfloat16)
    row_shape = (groups, per_device, capacity, model_width)
    send_tokens = (
        jnp.einsum("ts,td->sd", either, tokens, preferred_element_type=f32)
        .astype(jnp.bfloat16)
        .reshape(row_shape)
    )
    send_grads = (
        jnp.einsum("ts,td->sd", either, grad_out, preferred_element_type=f32)
        .astype(jnp.bfloat16)
        .reshape(row_shape)
    )
    send_probs = (
        jnp.einsum("tks,tk->s", slot_hits, route_probs.astype(f32), precision=high)
        .astype(jnp.bfloat16)
        .reshape(row_shape[:3])
    )
    recv_tokens, recv_grads, recv_probs = (
        lax.all_to_all(send_tokens, "expert", split_axis=0, concat_axis=0, tiled=True),
        lax.all_to_all(send_grads, "expert", split_axis=0, concat_axis=0, tiled=True),
        lax.all_to_all(send_probs, "expert", split_axis=0, concat_axis=0, tiled=True),
    )
    level_rows = jnp.repeat(lookup(gate_up_scale_index, scale_table), QBLOCK, axis=0)
    full_scale = jnp.repeat(level_rows, hidden, axis=2)
    down_scale = jnp.repeat(lookup(down_scale_index, scale_table), QBLOCK, axis=1)
    down_eff = (down_weight.astype(f32) * down_scale[:, :, None]).astype(jnp.bfloat16)
    gathered = lax.all_gather(gate_up_weight, "dp", axis=0, tiled=True)
    gate_up_eff = (gathered.astype(f32) * full_scale).astype(jnp.bfloat16)
    projected = jnp.einsum("sjcd,djf->sjcf", recv_tokens, gate_up_eff, preferred_element_type=f32)
    gate_part = projected[..., :hidden]
    up_part = projected[..., hidden:]
    sigmoid_gate = jax.nn.sigmoid(gate_part)
    activated = gate_part * sigmoid_gate
    hidden_rows = (activated * up_part).astype(jnp.bfloat16)
    hidden_grad = jnp.einsum("sjcd,jfd->sjcf", recv_grads, down_eff, preferred_element_type=f32)
    probs_wide = recv_probs.astype(f32)[..., None]
    scaled_grad = probs_wide * hidden_grad
    gate_grad = scaled_grad * up_part * sigmoid_gate * (1.0 + gate_part * (1.0 - sigmoid_gate))
    up_grad = scaled_grad * activated
    joint_grad = jnp.concatenate([gate_grad, up_grad], axis=-1).astype(jnp.bfloat16)
    row_grads = jnp.einsum(
        "sjcf,djf->sjcd", joint_grad, gate_up_eff, preferred_element_type=f32
    ).astype(jnp.bfloat16)
    back_rows = lax.all_to_all(row_grads, "expert", split_axis=0, concat_axis=0, tiled=True)
    token_grad = jnp.dot(
        either, back_rows.reshape(slots_all, model_width), preferred_element_type=f32
    ).astype(jnp.bfloat16)
    expert_out = jnp.einsum("sjcf,jfd->sjcd", hidden_rows, down_eff, preferred_element_type=f32)
    back_out = lax.all_to_all(
        expert_out.astype(jnp.bfloat16), "expert", split_axis=0, concat_axis=0, tiled=True
    ).astype(expert_out.dtype)
    picked = jnp.einsum(
        "tks,sd->tkd", slot_hits, back_out.reshape(slots_all, model_width), precision=high
    )
    prob_grad = jnp.sum(picked * grad_out.astype(f32)[:, None, :], axis=-1)
    weighted = (probs_wide * hidden_rows.astype(f32)).astype(jnp.bfloat16)
    partial_sum = jnp.einsum("sjcd,sjcf->djf", recv_tokens, joint_grad, preferred_element_type=f32)
    gate_up_grad = lax.psum_scatter(
        (partial_sum * full_scale).astype(jnp.bfloat16), "dp", scatter_dimension=0, tiled=True
    )
    down_part = (
        jnp.einsum("sjcf,sjcd->jfd", weighted, recv_grads, preferred_element_type=f32)
        * down_scale[:, :, None]
    )
    down_grad = lax.psum(down_part.astype(jnp.bfloat16), "dp")
    return (token_grad, prob_grad, gate_up_grad, down_grad)


def solution(mesh):
    in_specs = (
        P(("dp", "expert"), None),
        P(("dp", "expert"), None),
        P(("dp", "expert"), None),
        P(("dp", "expert"), None),
        P("dp", "expert", None),
        P("expert", None, None),
        P(None, "expert", None),
        P("expert", None),
        P(),
    )
    out_specs = (
        P(("dp", "expert"), None),
        P(("dp", "expert"), None),
        P("dp", "expert", None),
        P("expert", None, None),
    )
    return jax.shard_map(body, mesh=mesh, in_specs=in_specs, out_specs=out_specs, check_vma=False)
```

profile of v0, /device:TPU:2, one launch (start us, length us, event | category | flops | bytes accessed | tf_op | source)
XLA Modules:
  0.0 353.9 jit_solution(2334480392853353179)
XLA Ops:
  11.6 9.4 %all-to-all-start = ((bf16[32,1,16]{2,1,0:T(2,128)(2,1)}), bf16[32,1,16]{2,1,0:T(2,128)(2,1)S(1)}, u32[]{:S(2)}, u32[]{:S(2)}) async-start(bf16[32,1,16]{2,1,0:T(2,128)(2,1)} %reshape.246), calls=%async_computation | async-start | bytes 32768 | tf_op jit(solution)/shard_map/all_to_all | solution.py:74
  22.6 4.5 %all-to-all-done = bf16[32,1,16]{2,1,0:T(2,128)(2,1)S(1)} async-done(((bf16[32,1,16]{2,1,0:T(2,128)(2,1)}), bf16[32,1,16]{2,1,0:T(2,128)(2,1)S(1)}, u32[]{:S(2)}, u32[]{:S(2)}) %all-to-all-start) | async-done | bytes 1056 | tf_op jit(solution)/shard_map/all_to_all | solution.py:74
  27.2 5.7 %all-to-all-start.2 = ((bf16[32,1,16,1024]{3,2,1,0:T(8,128)(2,1)}), bf16[32,1,16,1024]{3,2,1,0:T(8,128)(2,1)}, u32[]{:S(2)}, u32[]{:S(2)}) async-start(bf16[32,1,16,1024]{3,2,1,0:T(8,128)(2,1)} %bitcast.19), calls=%async_computation.2 | async-start | bytes 2097152 | tf_op jit(solution)/shard_map/all_to_all | solution.py:72
  35.5 55.5 %all-gather.2.cloned.1.call-done = bf16[1024,1,1536]{2,0,1:T(8,128)(2,1)} async-done(((bf16[64,1,1536]{2,0,1:T(8,128)(2,1)}), bf16[1024,1,1536]{2,0,1:T(8,128)(2,1)}) %all-gather.2.cloned.1.call-update) | async-done | bytes 3145744 | tf_op jit(solution)/shard_map/all_gather | solution.py:80
  91.0 3.2 copy.76
  94.2 7.2 %all-to-all-start.1 = ((bf16[32,1,16,1024]{3,2,1,0:T(8,128)(2,1)}), bf16[32,1,16,1024]{3,2,1,0:T(8,128)(2,1)}, u32[]{:S(2)}, u32[]{:S(2)}) async-start(bf16[32,1,16,1024]{3,2,1,0:T(8,128)(2,1)} %bitcast.139), calls=%async_computation.1 | async-start | bytes 2097152 | tf_op jit(solution)/shard_map/all_to_all | solution.py:73
  103.7 1.7 copy-done.1
  105.4 1.7 copy-done.2
  107.1 5.1 %convolution_bitcast_fusion = f32[32,1,16,1536]{3,0,2,1:T(8,128)} fusion(bf16[1024,1536,1]{0,1,2:T(8,128)(2,1)S(1)} %fusion.3, bf16[32,1,16,1024]{3,2,1,0:T(8,128)(2,1)} %all-to-all-done.2), kind=kOutput, calls=%fused_computation.4 | convolution fusion | flops 1610612736 | bytes 7340032 | tf_op jit(solution)/shard_map/sjcd,djf->sjcf/dot_general | solution.py:82
  112.2 5.5 %all-to-all-done.1 = bf16[32,1,16,1024]{3,2,1,0:T(8,128)(2,1)} async-done(((bf16[32,1,16,1024]{3,2,1,0:T(8,128)(2,1)}), bf16[32,1,16,1024]{3,2,1,0:T(8,128)(2,1)}, u32[]{:S(2)}, u32[]{:S(2)}) %all-to-all-start.1) | async-done | bytes 1048608 | tf_op jit(solution)/shard_map/all_to_all | solution.py:73
  117.6 5.3 %fusion.31 = (bf16[32,16,768]{2,0,1:T(8,128)(2,1)S(1)}, bf16[32,16,768]{2,0,1:T(8,128)(2,1)S(1)}, bf16[32,1,16,768]{3,0,2,1:T(8,128)(2,1)}) fusion(f32[32,1,16,1536]{3,0,2,1:T(8,128)} %convolution_bitcast_fusion, bf16[32,1,16,1024]{3,2,1,0:T(8,128)(2,1)} %all-to-all-done.1, bf16[1,768,1024]{2,1,0:T(8,128)(2,1)S(1)} %copy-done.11, f32[768]{0:T(1024)S(1)} %copy-done.8, ...), kind=kOutput, calls=%fused_computation.49 | convolution fusion | flops 813957120 | bytes 8131584 | tf_op jit(solution)/shard_map/sjcd,jfd->sjcf/dot_general | solution.py:88
  123.0 3.8 %fusion.17 = f32[1536,1024,1]{1,0,2:T(8,128)S(1)} fusion(bf16[32,16,768]{2,0,1:T(8,128)(2,1)S(1)} %get-tuple-element.25, bf16[32,16,768]{2,0,1:T(8,128)(2,1)S(1)} %get-tuple-element.24, bf16[32,1,16,1024]{3,2,1,0:T(8,128)(2,1)} %all-to-all-done.2), kind=kOutput, calls=%fused_computation.36 | convolution fusion | flops 1613758464 | bytes 8912896 | tf_op jit(solution)/shard_map/sjcd,sjcf->djf/dot_general | solution.py:110
  126.8 1.8 fusion.2
  128.6 3.0 copy.96
  135.8 5.7 %all-to-all-start.4 = ((bf16[32,1,16,1024]{3,2,1,0:T(8,128)(2,1)}), bf16[32,1,16,1024]{3,2,1,0:T(8,128)(2,1)}, u32[]{:S(2)}, u32[]{:S(2)}) async-start(bf16[32,1,16,1024]{3,2,1,0:T(8,128)(2,1)} %copy.86), calls=%async_computation.4 | async-start | bytes 2097152 | tf_op jit(solution)/shard_map/all_to_all | solution.py:102
  141.8 4.1 %fusion.11 = bf16[1,768,1024]{2,1,0:T(8,128)(2,1)} fusion(f32[768]{0:T(1024)S(1)} %copy-done.8, bf16[32,1,16,1024]{3,2,1,0:T(8,128)(2,1)} %all-to-all-done.1, bf16[32,1,16,768]{3,0,2,1:T(8,128)(2,1)} %get-tuple-element.26, f32[32,16]{0,1:T(8,128)S(1)} %copy.78), kind=kOutput, calls=%fused_computation.23 | convolution fusion | flops 808058880 | bytes 3412992 | tf_op jit(solution)/shard_map/sjcf,sjcd->jfd/dot_general | solution.py:115
  146.0 3.2 fusion.13
  150.7 7.1 %all-to-all-done.4 = bf16[32,1,16,1024]{3,2,1,0:T(8,128)(2,1)} async-done(((bf16[32,1,16,1024]{3,2,1,0:T(8,128)(2,1)}), bf16[32,1,16,1024]{3,2,1,0:T(8,128)(2,1)}, u32[]{:S(2)}, u32[]{:S(2)}) %all-to-all-start.4) | async-done | bytes 1048608 | tf_op jit(solution)/shard_map/all_to_all | solution.py:102
  157.8 5.0 %all-to-all-start.3 = ((bf16[32,1,16,1024]{3,2,1,0:T(8,128)(2,1)}), bf16[32,1,16,1024]{3,2,1,0:T(8,128)(2,1)S(1)}, u32[]{:S(2)}, u32[]{:S(2)}) async-start(bf16[32,1,16,1024]{3,2,1,0:T(8,128)(2,1)} %copy.85), calls=%async_computation.3 | async-start | bytes 2097152 | tf_op jit(solution)/shard_map/all_to_all | solution.py:97
  162.9 2.4 fusion.14
  165.3 13.8 %all-to-all-done.3 = bf16[32,1,16,1024]{3,2,1,0:T(8,128)(2,1)S(1)} async-done(((bf16[32,1,16,1024]{3,2,1,0:T(8,128)(2,1)}), bf16[32,1,16,1024]{3,2,1,0:T(8,128)(2,1)S(1)}, u32[]{:S(2)}, u32[]{:S(2)}) %all-to-all-start.3) | async-done | bytes 1048608 | tf_op jit(solution)/shard_map/all_to_all | solution.py:97
  180.1 22.4 %reduce-scatter.4.cloned.1.call-done = bf16[64,1536]{1,0:T(8,128)(2,1)} async-done(((bf16[1024,1536]{1,0:T(8,128)(2,1)}), bf16[64,1536]{1,0:T(8,128)(2,1)}) %reduce-scatter.4.cloned.1.call-update) | async-done | bytes 196624
  204.5 140.2 %all-reduce.2.cloned.1.call-done = bf16[1,768,1024]{2,1,0:T(8,128)(2,1)} async-done(((bf16[1,768,1024]{2,1,0:T(8,128)(2,1)}), bf16[1,768,1024]{2,1,0:T(8,128)(2,1)}) %all-reduce.2.cloned.1.call-update) | async-done | bytes 1572880 | tf_op jit(solution)/shard_map/psum | solution.py:118
  344.7 2.7 copy.122
  (73 shorter events, 20.0 us)
Async XLA Ops:
  7.2 14.0 %copy-start = (bf16[128,1024]{1,0:T(8,128)(2,1)S(1)}, bf16[128,1024]{1,0:T(8,128)(2,1)}, u32[]{:S(2)}) copy-start(bf16[128,1024]{1,0:T(8,128)(2,1)} %param.9) | copy-start | bytes 786436
  7.2 83.9 %all-gather.2.cloned.1.call-start = ((), (), s32[]{:S(2)}) async-start(), calls=%async_computation.6 | async-start | bytes 3342336 | tf_op jit(solution)/shard_map/all_gather | solution.py:80
  10.0 11.0 %copy-start.6 = (s32[128,2]{0,1:T(2,128)}, s32[128,2]{0,1:T(2,128)S(1)}, u32[]{:S(2)}) copy-start(s32[128,2]{0,1:T(2,128)S(1)} %multiply_add_fusion) | copy-start | bytes 3076
  11.6 15.6 %all-to-all-start = ((bf16[32,1,16]{2,1,0:T(2,128)(2,1)}), bf16[32,1,16]{2,1,0:T(2,128)(2,1)S(1)}, u32[]{:S(2)}, u32[]{:S(2)}) async-start(bf16[32,1,16]{2,1,0:T(2,128)(2,1)} %reshape.246), calls=%async_computation | async-start | bytes 32768 | tf_op jit(solution)/shard_map/all_to_all | solution.py:74
  21.1 11.8 %copy-start.9 = (s32[8,1,2]{0,2,1:T(2,128)S(1)}, s32[8,1,2]{0,2,1:T(2,128)}, u32[]{:S(2)}) copy-start(s32[8,1,2]{0,2,1:T(2,128)} %param.15) | copy-start | bytes 196
  21.1 11.8 %copy-start.10 = (f32[16]{0:T(128)S(1)}, f32[16]{0:T(128)}, u32[]{:S(2)}) copy-start(f32[16]{0:T(128)} %param.17) | copy-start | bytes 196
  21.1 12.0 %copy-start.13 = (s32[1,6]{1,0:T(1,128)S(1)}, s32[1,6]{1,0:T(1,128)}, u32[]{:S(2)}) copy-start(s32[1,6]{1,0:T(1,128)} %param.16) | copy-start | bytes 76
  21.2 12.9 %copy-start.4 = (bf16[128,1024]{1,0:T(8,128)(2,1)S(1)}, bf16[128,1024]{1,0:T(8,128)(2,1)}, u32[]{:S(2)}) copy-start(bf16[128,1024]{1,0:T(8,128)(2,1)} %param.10) | copy-start | bytes 786436
  27.2 67.1 %all-to-all-start.2 = ((bf16[32,1,16,1024]{3,2,1,0:T(8,128)(2,1)}), bf16[32,1,16,1024]{3,2,1,0:T(8,128)(2,1)}, u32[]{:S(2)}, u32[]{:S(2)}) async-start(bf16[32,1,16,1024]{3,2,1,0:T(8,128)(2,1)} %bitcast.19), calls=%async_computation.2 | async-start | bytes 2097152 | tf_op jit(solution)/shard_map/all_to_all | solution.py:72
  94.2 23.4 %all-to-all-start.1 = ((bf16[32,1,16,1024]{3,2,1,0:T(8,128)(2,1)}), bf16[32,1,16,1024]{3,2,1,0:T(8,128)(2,1)}, u32[]{:S(2)}, u32[]{:S(2)}) async-start(bf16[32,1,16,1024]{3,2,1,0:T(8,128)(2,1)} %bitcast.139), calls=%async_computation.1 | async-start | bytes 2097152 | tf_op jit(solution)/shard_map/all_to_all | solution.py:73
  101.5 101.0 %reduce-scatter.4.cloned.1.call-start = ((), (), s32[]{:S(2)}) async-start(), calls=%async_computation.8 | async-start | bytes 3342336
  102.5 2.9 copy-start.1
  107.1 10.6 %copy-start.8 = (f32[768]{0:T(1024)S(1)}, f32[768]{0:T(1024)}, u32[]{:S(2)}) copy-start(f32[768]{0:T(1024)} %broadcast_bitcast_fusion.1) | copy-start | bytes 9220
  107.1 10.6 %copy-start.11 = (bf16[1,768,1024]{2,1,0:T(8,128)(2,1)S(1)}, bf16[1,768,1024]{2,1,0:T(8,128)(2,1)}, u32[]{:S(2)}) copy-start(bf16[1,768,1024]{2,1,0:T(8,128)(2,1)} %param.14) | copy-start | bytes 4718596
  117.6 9.2 %slice-start = ((s8[6291456]{0:T(1024)(128)(4,1)}), s8[4194304]{0:T(1024)(128)(4,1)S(1)}, s32[]{:S(2)}) async-start(s8[6291456]{0:T(1024)(128)(4,1)} %bitcast.136), calls=%async_computation.9 | async-start | bytes 8388608
  122.9 3.8 %copy-start.15 = (bf16[32,16,768]{2,0,1:T(8,128)(2,1)}, bf16[32,16,768]{2,0,1:T(8,128)(2,1)S(1)}, u32[]{:S(2)}) copy-start(bf16[32,16,768]{2,0,1:T(8,128)(2,1)S(1)} %get-tuple-element.24) | copy-start | bytes 2359300
  122.9 3.8 %copy-start.16 = (bf16[32,16,768]{2,0,1:T(8,128)(2,1)}, bf16[32,16,768]{2,0,1:T(8,128)(2,1)S(1)}, u32[]{:S(2)}) copy-start(bf16[32,16,768]{2,0,1:T(8,128)(2,1)S(1)} %get-tuple-element.25) | copy-start | bytes 2359300
  123.0 3.9 %slice-start.1 = ((s8[6291456]{0:T(1024)(128)(4,1)}), s8[2097152]{0:T(1024)(128)(4,1)S(1)}, s32[]{:S(2)}) async-start(s8[6291456]{0:T(1024)(128)(4,1)} %bitcast.136), calls=%async_computation.10 | async-start | bytes 4194304
  135.8 22.0 %all-to-all-start.4 = ((bf16[32,1,16,1024]{3,2,1,0:T(8,128)(2,1)}), bf16[32,1,16,1024]{3,2,1,0:T(8,128)(2,1)}, u32[]{:S(2)}, u32[]{:S(2)}) async-start(bf16[32,1,16,1024]{3,2,1,0:T(8,128)(2,1)} %copy.86), calls=%async_computation.4 | async-start | bytes 2097152 | tf_op jit(solution)/shard_map/all_to_all | solution.py:102
  141.6 4.4 %copy-start.3 = (bf16[1024,1536,1]{0,1,2:T(8,128)(2,1)S(1)}, bf16[1024,1536,1]{0,1,2:T(8,128)(2,1)}, u32[]{:S(2)}) copy-start(bf16[1024,1536,1]{0,1,2:T(8,128)(2,1)} %copy-done.2) | copy-start | bytes 9437188
  141.6 203.2 %all-reduce.2.cloned.1.call-start = ((), (), s32[]{:S(2)}) async-start(), calls=%async_computation.7 | async-start | bytes 3145728 | tf_op jit(solution)/shard_map/psum | solution.py:118
  149.1 13.7 %copy-start.5 = (bf16[128,1024]{1,0:T(8,128)(2,1)S(1)}, bf16[128,1024]{1,0:T(8,128)(2,1)}, u32[]{:S(2)}) copy-start(bf16[128,1024]{1,0:T(8,128)(2,1)} %param.10) | copy-start | bytes 786436
  149.1 13.8 %copy-start.7 = (s32[128,2]{0,1:T(2,128)S(1)}, s32[128,2]{0,1:T(2,128)}, u32[]{:S(2)}) copy-start(s32[128,2]{0,1:T(2,128)} %copy-done.6) | copy-start | bytes 3076
  157.8 21.3 %all-to-all-start.3 = ((bf16[32,1,16,1024]{3,2,1,0:T(8,128)(2,1)}), bf16[32,1,16,1024]{3,2,1,0:T(8,128)(2,1)S(1)}, u32[]{:S(2)}, u32[]{:S(2)}) async-start(bf16[32,1,16,1024]{3,2,1,0:T(8,128)(2,1)} %copy.85), calls=%async_computation.3 | async-start | bytes 2097152 | tf_op jit(solution)/shard_map/all_to_all | solution.py:97
  (3 other events, 4.7 us)
Sparse Core Ops, SparseCore 0:
  10.1 80.9 all-gather.1
  131.7 70.7 reduce-scatter.3
  205.4 139.2 all-reduce.1
where the time goes:
time: 355 us; the launch traced here: 354 us
  waiting for transfers between devices  250 us (70%)
  starting transfers between devices  33.6 us (9%)
  matrix products  29.9 us (8%)
  local copies, waits for them, and re-layouts  22.4 us (6%)
  between operations  14.1 us (4%)
  other arithmetic  4.22 us (1%)
    psum x1, waiting for transfers between devices, body(): down_grad = lax.psum(down_part.astype(jnp.bfloat16), 'dp')  140 us
    all_gather x1, waiting for transfers between devices, body(): gathered = lax.all_gather(gate_up_weight, 'dp', axis=0, tiled=True)  55.5 us
    unnamed x4, waiting for transfers between devices  23.1 us
    all_to_all x1, waiting for transfers between devices, body(): lax.all_to_all(row_grads, 'expert', split_axis=0, concat_axis=0, tiled=True)  13.8 us
    unnamed x45, local copies, waits for them, and re-layouts  13.5 us
    all_to_all x1, starting transfers between devices, body(): lax.all_to_all(send_probs, 'expert', split_axis=0, concat_axis=0, tiled=T...  9.4 us
    all_to_all x1, starting transfers between devices, body(): lax.all_to_all(send_grads, 'expert', split_axis=0, concat_axis=0, tiled=T...  7.21 us
    all_to_all x1, waiting for transfers between devices, body(): lax.all_to_all(expert_out.astype(jnp.bfloat16), 'expert', split_axis=0, c...  7.1 us
  transfers between devices with their start and end apart: 8, of which 7 were waited for; matrix products, arithmetic and copies ran while one was open for 10% of the time, Pallas kernels for 0%

commit v1 on v0

--- a/solution.py
+++ b/solution.py
@@ -115,7 +115,7 @@
         jnp.einsum("sjcf,sjcd->jfd", weighted, recv_grads, preferred_element_type=f32)
         * down_scale[:, :, None]
     )
-    down_grad = lax.psum(down_part.astype(jnp.bfloat16), "dp")
+    down_grad = jnp.sum(lax.all_gather(down_part.astype(jnp.bfloat16), "dp"), axis=0)
     return (token_grad, prob_grad, gate_up_grad, down_grad)
 
 

time: 355 us -> 501 us (1.41)
  the two profiles are of different devices: /device:TPU:2 before, /device:TPU:1 now
where the time goes in v1:
time: 501 us; the launch traced here: 500 us
  waiting for transfers between devices  377 us (75%)
  starting transfers between devices  40.6 us (8%)
  matrix products  29.6 us (6%)
  other arithmetic  19.1 us (4%)
  local copies, waits for them, and re-layouts  18.7 us (4%)
  between operations  14.1 us (3%)
    all_gather x1, waiting for transfers between devices, body(): lax.all_gather(down_part.astype(jnp.bfloat16), 'dp')  281 us
    all_gather x1, waiting for transfers between devices, body(): gathered = lax.all_gather(gate_up_weight, 'dp', axis=0, tiled=True)  47 us
    all_to_all x1, starting transfers between devices, body(): lax.all_to_all(send_grads, 'expert', split_axis=0, concat_axis=0, tiled=T...  16.3 us
    reduce_sum x1, other arithmetic, body(): jnp.sum(lax.all_gather(down_part.astype(jnp.bfloat16), 'dp'), axis=0)  14.9 us
    all_to_all x1, waiting for transfers between devices, body(): lax.all_to_all(row_grads, 'expert', split_axis=0, concat_axis=0, tiled=True)  14.9 us
    all_to_all x1, waiting for transfers between devices, body(): lax.all_to_all(expert_out.astype(jnp.bfloat16), 'expert', split_axis=0, c...  12.5 us
    all_to_all x1, starting transfers between devices, body(): lax.all_to_all(send_probs, 'expert', split_axis=0, concat_axis=0, tiled=T...  10.4 us
    unnamed x40, local copies, waits for them, and re-layouts  10.4 us
  transfers between devices with their start and end apart: 8, of which 7 were waited for; matrix products, arithmetic and copies ran while one was open for 7% of the time, Pallas kernels for 0%

profile of v1, /device:TPU:1, one launch (start us, length us, event | category | flops | bytes accessed | tf_op | source)
XLA Modules:
  0.0 499.6 jit_solution(4482076182277232123)
XLA Ops:
  11.6 10.4 %all-to-all-start = ((bf16[32,1,16]{2,1,0:T(2,128)(2,1)}), bf16[32,1,16]{2,1,0:T(2,128)(2,1)S(1)}, u32[]{:S(2)}, u32[]{:S(2)}) async-start(bf16[32,1,16]{2,1,0:T(2,128)(2,1)} %reshape.250), calls=%async_computation | async-start | bytes 32768 | tf_op jit(solution)/shard_map/all_to_all | solution.py:74
  23.6 5.3 %all-to-all-done = bf16[32,1,16]{2,1,0:T(2,128)(2,1)S(1)} async-done(((bf16[32,1,16]{2,1,0:T(2,128)(2,1)}), bf16[32,1,16]{2,1,0:T(2,128)(2,1)S(1)}, u32[]{:S(2)}, u32[]{:S(2)}) %all-to-all-start) | async-done | bytes 1056 | tf_op jit(solution)/shard_map/all_to_all | solution.py:74
  28.9 4.9 all-to-all-start.2
  35.9 47.0 %all-gather.4.cloned.1.call-done = bf16[1024,1,1536]{2,0,1:T(8,128)(2,1)} async-done(((bf16[64,1,1536]{2,0,1:T(8,128)(2,1)}), bf16[1024,1,1536]{2,0,1:T(8,128)(2,1)}) %all-gather.4.cloned.1.call-update) | async-done | bytes 3145744 | tf_op jit(solution)/shard_map/all_gather | solution.py:80
  83.0 3.2 copy.76
  86.2 16.3 %all-to-all-start.1 = ((bf16[32,1,16,1024]{3,2,1,0:T(8,128)(2,1)}), bf16[32,1,16,1024]{3,2,1,0:T(8,128)(2,1)}, u32[]{:S(2)}, u32[]{:S(2)}) async-start(bf16[32,1,16,1024]{3,2,1,0:T(8,128)(2,1)} %bitcast.138), calls=%async_computation.1 | async-start | bytes 2097152 | tf_op jit(solution)/shard_map/all_to_all | solution.py:73
  104.7 1.7 copy-done.2
  106.3 1.7 copy-done.3
  108.0 5.1 %convolution_bitcast_fusion = f32[32,1,16,1536]{3,0,2,1:T(8,128)} fusion(bf16[1024,1536,1]{0,1,2:T(8,128)(2,1)S(1)} %fusion.3, bf16[32,1,16,1024]{3,2,1,0:T(8,128)(2,1)} %all-to-all-done.2), kind=kOutput, calls=%fused_computation.4 | convolution fusion | flops 1610612736 | bytes 7340032 | tf_op jit(solution)/shard_map/sjcd,djf->sjcf/dot_general | solution.py:82
  113.2 6.5 %all-to-all-done.1 = bf16[32,1,16,1024]{3,2,1,0:T(8,128)(2,1)} async-done(((bf16[32,1,16,1024]{3,2,1,0:T(8,128)(2,1)}), bf16[32,1,16,1024]{3,2,1,0:T(8,128)(2,1)}, u32[]{:S(2)}, u32[]{:S(2)}) %all-to-all-start.1) | async-done | bytes 1048608 | tf_op jit(solution)/shard_map/all_to_all | solution.py:73
  119.7 5.3 %fusion.30 = (bf16[32,16,768]{2,0,1:T(8,128)(2,1)S(1)}, bf16[32,16,768]{2,0,1:T(8,128)(2,1)S(1)}, bf16[32,1,16,768]{3,0,2,1:T(8,128)(2,1)}) fusion(f32[32,1,16,1536]{3,0,2,1:T(8,128)} %convolution_bitcast_fusion, bf16[32,1,16,1024]{3,2,1,0:T(8,128)(2,1)} %all-to-all-done.1, bf16[1,768,1024]{2,1,0:T(8,128)(2,1)S(1)} %copy-done.9, ...), kind=kOutput, calls=%fused_computation.48 | convolution fusion | flops 813957120 | bytes 8131584 | tf_op jit(solution)/shard_map/sjcd,jfd->sjcf/dot_general | solution.py:88
  125.0 3.8 fusion.16
  128.8 1.8 fusion.2
  130.6 3.0 copy.96
  134.7 3.7 fusion.4
  141.1 4.9 all-to-all-start.4
  146.0 3.2 fusion.12
  150.8 12.5 %all-to-all-done.4 = bf16[32,1,16,1024]{3,2,1,0:T(8,128)(2,1)} async-done(((bf16[32,1,16,1024]{3,2,1,0:T(8,128)(2,1)}), bf16[32,1,16,1024]{3,2,1,0:T(8,128)(2,1)}, u32[]{:S(2)}, u32[]{:S(2)}) %all-to-all-start.4) | async-done | bytes 1048608 | tf_op jit(solution)/shard_map/all_to_all | solution.py:102
  163.3 4.0 all-to-all-start.3
  167.4 2.4 fusion.13
  169.7 14.9 %all-to-all-done.3 = bf16[32,1,16,1024]{3,2,1,0:T(8,128)(2,1)S(1)} async-done(((bf16[32,1,16,1024]{3,2,1,0:T(8,128)(2,1)}), bf16[32,1,16,1024]{3,2,1,0:T(8,128)(2,1)S(1)}, u32[]{:S(2)}, u32[]{:S(2)}) %all-to-all-start.3) | async-done | bytes 1048608 | tf_op jit(solution)/shard_map/all_to_all | solution.py:97
  185.6 9.6 %reduce-scatter.4.cloned.1.call-done = bf16[64,1536]{1,0:T(8,128)(2,1)} async-done(((bf16[1024,1536]{1,0:T(8,128)(2,1)}), bf16[64,1536]{1,0:T(8,128)(2,1)}) %reduce-scatter.4.cloned.1.call-update) | async-done | bytes 196624
  197.2 280.9 %all-gather.6.cloned.1.call-done = bf16[12288,1024]{1,0:T(8,128)(2,1)} async-done(((bf16[768,1024]{1,0:T(8,128)(2,1)}), bf16[12288,1024]{1,0:T(8,128)(2,1)}) %all-gather.6.cloned.1.call-update) | async-done | bytes 25165840 | tf_op jit(solution)/shard_map/all_gather | solution.py:118
  478.1 14.9 %reduce.4 = bf16[768,1024]{1,0:T(8,128)(2,1)} reduce(bf16[16,768,1024]{2,1,0:T(8,128)(2,1)} %bitcast.137, bf16[]{:T(256)} %constant.12.clone.1), dimensions={0}, to_apply=%region_5.0 | reduce | flops 11796480 | bytes 26738690 | tf_op jit(solution)/shard_map/reduce_sum | solution.py:118
  (69 shorter events, 18.7 us)
Async XLA Ops:
  7.2 15.0 %copy-start = (bf16[128,1024]{1,0:T(8,128)(2,1)S(1)}, bf16[128,1024]{1,0:T(8,128)(2,1)}, u32[]{:S(2)}) copy-start(bf16[128,1024]{1,0:T(8,128)(2,1)} %param.9) | copy-start | bytes 786436
  7.2 75.8 %all-gather.4.cloned.1.call-start = ((), (), s32[]{:S(2)}) async-start(), calls=%async_computation.6 | async-start | bytes 3342336 | tf_op jit(solution)/shard_map/all_gather | solution.py:80
  11.6 17.3 %all-to-all-start = ((bf16[32,1,16]{2,1,0:T(2,128)(2,1)}), bf16[32,1,16]{2,1,0:T(2,128)(2,1)S(1)}, u32[]{:S(2)}, u32[]{:S(2)}) async-start(bf16[32,1,16]{2,1,0:T(2,128)(2,1)} %reshape.250), calls=%async_computation | async-start | bytes 32768 | tf_op jit(solution)/shard_map/all_to_all | solution.py:74
  22.1 11.8 %copy-start.7 = (s32[8,1,2]{0,2,1:T(2,128)S(1)}, s32[8,1,2]{0,2,1:T(2,128)}, u32[]{:S(2)}) copy-start(s32[8,1,2]{0,2,1:T(2,128)} %param.15) | copy-start | bytes 196
  22.1 11.8 %copy-start.8 = (f32[16]{0:T(128)S(1)}, f32[16]{0:T(128)}, u32[]{:S(2)}) copy-start(f32[16]{0:T(128)} %param.17) | copy-start | bytes 196
  22.1 12.0 %copy-start.11 = (s32[1,6]{1,0:T(1,128)S(1)}, s32[1,6]{1,0:T(1,128)}, u32[]{:S(2)}) copy-start(s32[1,6]{1,0:T(1,128)} %param.16) | copy-start | bytes 76
  22.1 12.3 %copy-start.5 = (bf16[128,1024]{1,0:T(8,128)(2,1)S(1)}, bf16[128,1024]{1,0:T(8,128)(2,1)}, u32[]{:S(2)}) copy-start(bf16[128,1024]{1,0:T(8,128)(2,1)} %param.10) | copy-start | bytes 786436
  28.9 57.2 %all-to-all-start.2 = ((bf16[32,1,16,1024]{3,2,1,0:T(8,128)(2,1)}), bf16[32,1,16,1024]{3,2,1,0:T(8,128)(2,1)}, u32[]{:S(2)}, u32[]{:S(2)}) async-start(bf16[32,1,16,1024]{3,2,1,0:T(8,128)(2,1)} %bitcast.19), calls=%async_computation.2 | async-start | bytes 2097152 | tf_op jit(solution)/shard_map/all_to_all | solution.py:72
  86.2 33.5 %all-to-all-start.1 = ((bf16[32,1,16,1024]{3,2,1,0:T(8,128)(2,1)}), bf16[32,1,16,1024]{3,2,1,0:T(8,128)(2,1)}, u32[]{:S(2)}, u32[]{:S(2)}) async-start(bf16[32,1,16,1024]{3,2,1,0:T(8,128)(2,1)} %bitcast.138), calls=%async_computation.1 | async-start | bytes 2097152 | tf_op jit(solution)/shard_map/all_to_all | solution.py:73
  102.4 92.8 %reduce-scatter.4.cloned.1.call-start = ((), (), s32[]{:S(2)}) async-start(), calls=%async_computation.8 | async-start | bytes 3342336
  103.4 2.9 copy-start.2
  106.3 1.7 copy-start.3
  108.0 11.6 %copy-start.9 = (bf16[1,768,1024]{2,1,0:T(8,128)(2,1)S(1)}, bf16[1,768,1024]{2,1,0:T(8,128)(2,1)}, u32[]{:S(2)}) copy-start(bf16[1,768,1024]{2,1,0:T(8,128)(2,1)} %param.14) | copy-start | bytes 4718596
  119.7 9.2 %slice-start = ((s8[6291456]{0:T(1024)(128)(4,1)}), s8[4194304]{0:T(1024)(128)(4,1)S(1)}, s32[]{:S(2)}) async-start(s8[6291456]{0:T(1024)(128)(4,1)} %bitcast.134), calls=%async_computation.9 | async-start | bytes 8388608
  124.9 3.8 copy-start.13
  124.9 3.8 copy-start.14
  124.9 3.9 slice-start.1
  133.6 344.5 %all-gather.6.cloned.1.call-start = ((), (), s32[]{:S(2)}) async-start(), calls=%async_computation.7 | async-start | bytes 26738688 | tf_op jit(solution)/shard_map/all_gather | solution.py:118
  134.7 3.7 copy-start.10
  139.6 6.4 %copy-start.4 = (bf16[1024,1536,1]{0,1,2:T(8,128)(2,1)S(1)}, bf16[1024,1536,1]{0,1,2:T(8,128)(2,1)}, u32[]{:S(2)}) copy-start(bf16[1024,1536,1]{0,1,2:T(8,128)(2,1)} %copy-done.3) | copy-start | bytes 9437188
  141.1 22.2 %all-to-all-start.4 = ((bf16[32,1,16,1024]{3,2,1,0:T(8,128)(2,1)}), bf16[32,1,16,1024]{3,2,1,0:T(8,128)(2,1)}, u32[]{:S(2)}, u32[]{:S(2)}) async-start(bf16[32,1,16,1024]{3,2,1,0:T(8,128)(2,1)} %copy.86), calls=%async_computation.4 | async-start | bytes 2097152 | tf_op jit(solution)/shard_map/all_to_all | solution.py:102
  149.2 18.1 %copy-start.6 = (bf16[128,1024]{1,0:T(8,128)(2,1)S(1)}, bf16[128,1024]{1,0:T(8,128)(2,1)}, u32[]{:S(2)}) copy-start(bf16[128,1024]{1,0:T(8,128)(2,1)} %param.10) | copy-start | bytes 786436
  163.3 21.3 %all-to-all-start.3 = ((bf16[32,1,16,1024]{3,2,1,0:T(8,128)(2,1)}), bf16[32,1,16,1024]{3,2,1,0:T(8,128)(2,1)S(1)}, u32[]{:S(2)}, u32[]{:S(2)}) async-start(bf16[32,1,16,1024]{3,2,1,0:T(8,128)(2,1)} %copy.85), calls=%async_computation.3 | async-start | bytes 2097152 | tf_op jit(solution)/shard_map/all_to_all | solution.py:97
  478.1 14.9 %copy-start.1 = (bf16[128,1024]{1,0:T(8,128)(2,1)S(1)}, bf16[128,1024]{1,0:T(8,128)(2,1)}, u32[]{:S(2)}) copy-start(bf16[128,1024]{1,0:T(8,128)(2,1)} %param.9) | copy-start | bytes 786436
  (1 other events, 1.1 us)
Sparse Core Ops, SparseCore 0:
  10.1 72.8 all-gather.3
  133.8 61.3 reduce-scatter.3
  197.8 280.2 all-gather.5
